TPU v7x, 32 devices: a whole 2x2x4 slice. The times are simulated.
32 devices in a mesh: ctx: 16 (over z, y, core), head: 2 (over x).
Axes of the slice: x: 2, y: 2, z: 4, core: 2. Of those that a mesh axis runs over, the one named last changes fastest.
Arguments:
- queries_nope: bfloat16 [1024, 8192], P('ctx', 'head'), may hold values from -4 to 4
- queries_rope: bfloat16 [1024, 4096], P('ctx', 'head'), may hold values from -128 to 128
- latents: bfloat16 [1024, 512], P('ctx'), may hold values from -8 to 8
- rope_keys: bfloat16 [1024, 64], P('ctx'), may hold values from -4 to 4
- positions: int32 [1024], P('ctx'), may hold values from 0 to 1535
- key_up: bfloat16 [512, 8192], P(None, 'head'), may hold values from -0.5 to 0.5
- value_up: bfloat16 [512, 8192], P(None, 'head'), may hold values from -0.25 to 0.25
- out_proj: bfloat16 [8192, 3584], P('head', 'ctx'), may hold values from -0.0625 to 0.0625
Outputs:
- attended: bfloat16 [1024, 3584], P('ctx', 'head')
All inputs are finite; a program needn't handle non-finite values.
Results may differ from a plain program's by a relative error of at most 0.014.
The roundings to bfloat16 on the way count: a program that leaves them out, or rounds other values in their place, can miss the bound.
Values may be sent and summed in bfloat16 or wider, within the bound.
A program may use at most 128 MiB of HBM per device.

v0:
```python
import functools
import math

import jax
import jax.numpy as jnp
from jax import lax
from jax.experimental import pallas as pl
from jax.experimental.pallas import tpu as pltpu
from jax.sharding import PartitionSpec as P

LATENT = 512
ROPE = 64
NOPE = 128
VDIM = 128
KEYW = 640
CORES = 2
LINES = 2
GROUP = 8
SPLIT = 2
CHUNKS = 4
LAG = 1

masked_value = -1e30
MESH = pl.DeviceIdType.MESH
NT = (((1,), (1,)), ((), ()))


def rope_tables(token_pos, width):
    half_width = width // 2
    freqs = jnp.exp(jnp.arange(half_width, dtype=jnp.float32) * (-2.0 * math.log(10000.0) / width))
    angle = token_pos.astype(jnp.float32)[:, None] * freqs[None, :]
    return (jnp.cos(angle), jnp.sin(angle))


def swap_halves(values):
    lane = lax.broadcasted_iota(jnp.int32, values.shape, 1)
    ahead = pltpu.roll(values, 2 * ROPE - ROPE // 2, 1)
    behind = pltpu.roll(values, ROPE // 2, 1)
    return jnp.where(lax.rem(lane, ROPE) < ROPE // 2, ahead, behind)


def kernel(
    n_ctx,
    n_head,
    lat_hbm,
    rk_hbm,
    cos_ref,
    sin_ref,
    qn_hbm,
    qr_hbm,
    key_up_hbm,
    value_up_hbm,
    proj_hbm,
    out_ref,
    lat_ref,
    rk_ref,
    wide,
    qn_ref,
    qr_ref,
    key_up,
    value_up,
    proj,
    kv,
    query,
    ho,
    acc,
    out_send,
    land,
    load_sem,
    proj_send_c,
    proj_send_y,
    proj_send_d,
    proj_recv_c,
    proj_recv_y,
    proj_recv_d,
    kv_send_z,
    kv_send_y,
    kv_send_c,
    kv_recv,
    ho_send_z,
    ho_recv,
    back_send,
    land_recv,
):
    tokens = lat_ref.shape[0]
    n_z = n_ctx // (CORES * LINES)
    sub = tokens // SPLIT
    ticks = ho.shape[0]
    groups = ticks // SPLIT
    depth = proj_hbm.shape[1]
    spots = land.shape[1]
    me = lax.axis_index("ctx")
    head = lax.axis_index("head")
    core = lax.rem(me, CORES)
    line = lax.rem(me // CORES, LINES)
    z = me // (CORES * LINES)
    other_line = 1 - line
    owner_head = z // spots
    slot = lax.rem(z, spots)

    def ctx_of(z_at, line_at, core_at):
        return (z_at * LINES + line_at) * CORES + core_at

    core_peer = (ctx_of(z, line, 1 - core), head)
    line_peer = (ctx_of(z, other_line, core), head)

    def z_peer(step):
        return lax.rem(z + step, n_z)

    barrier = pltpu.get_barrier_semaphore()
    n_class = (n_ctx // CORES) * n_head
    mine = (me // CORES) * n_head + head

    def greet(step, carry):
        other = lax.rem(mine + step, n_class)
        there = ((other // n_head) * CORES + core, lax.rem(other, n_head))
        pl.semaphore_signal(barrier, inc=1, device_id=there, device_id_type=MESH)
        return carry

    lax.fori_loop(1, n_class, greet, 0)
    pl.semaphore_signal(barrier, inc=1, device_id=core_peer, device_id_type=MESH)

    loads = []
    for source, target in (
        (lat_hbm, lat_ref),
        (rk_hbm, rk_ref),
        (qn_hbm, qn_ref),
        (qr_hbm, qr_ref),
        (key_up_hbm, key_up),
        (value_up_hbm, value_up),
        (proj_hbm, proj.at[line, core]),
    ):
        loads.append(pltpu.make_async_copy(source, target, load_sem.at[len(loads)]))
        loads[-1].start()
    load_lat, load_rk, load_qn, load_qr, load_key, load_value, load_proj = loads
    wide[...] = jnp.zeros_like(wide)
    load_lat.wait()
    load_rk.wait()
    wide[:, pl.ds(0, ROPE)] = rk_ref[...].astype(jnp.float32)
    pl.semaphore_wait(barrier, n_class)

    def kv_copy(src, origin, send_sem, there):
        return pltpu.make_async_remote_copy(
            src_ref=src,
            dst_ref=kv.at[origin],
            send_sem=send_sem,
            recv_sem=kv_recv.at[origin],
            device_id=there,
            device_id_type=MESH,
        )

    def rotated(values):
        values = values.astype(jnp.float32)
        return values * cos_ref[...] + swap_halves(values) * sin_ref[...]

    kv[me, :, pl.ds(0, LATENT)] = lat_ref[...]
    kv[me, :, pl.ds(LATENT, KEYW - LATENT)] = rotated(wide[...]).astype(jnp.bfloat16)

    sends = []

    def send_if(allowed, origin, send_sem, there):
        copy = kv_copy(kv.at[origin], origin, send_sem, there)
        sends.append((allowed, copy))
        if allowed is None:
            copy.start()
        else:
            pl.when(allowed)(copy.start)

    for step in range(1, n_z):
        there = (ctx_of(lax.rem(z + step, n_z), line, core), head)
        send_if(z + step < n_z, me, kv_send_z.at[step - 1], there)
    send_if(None, me, kv_send_y.at[0], line_peer)
    send_if(None, me, kv_send_c.at[0, 0], core_peer)
    for step in range(1, n_z):

        @pl.when(z + step < n_z)
        def _():
            later = pl.ds((z + step) * (LINES * CORES), LINES * CORES)
            kv[later] = jnp.zeros((LINES * CORES, tokens, KEYW), jnp.bfloat16)

    def chunk_of(index):
        return pl.ds(index * (depth // CHUNKS), depth // CHUNKS)

    proj_core = pltpu.make_async_remote_copy(
        src_ref=proj_hbm,
        dst_ref=proj.at[line, core],
        send_sem=proj_send_c,
        recv_sem=proj_recv_c,
        device_id=core_peer,
        device_id_type=MESH,
    )

    def proj_line(index):
        return pltpu.make_async_remote_copy(
            src_ref=proj_hbm.at[:, chunk_of(index)],
            dst_ref=proj.at[line, core, :, chunk_of(index)],
            send_sem=proj_send_y.at[index],
            recv_sem=proj_recv_y.at[index],
            device_id=line_peer,
            device_id_type=MESH,
        )

    def proj_across(index):
        return pltpu.make_async_remote_copy(
            src_ref=proj.at[other_line, core, :, chunk_of(index)],
            dst_ref=proj.at[other_line, core, :, chunk_of(index)],
            send_sem=proj_send_d.at[index],
            recv_sem=proj_recv_d.at[index],
            device_id=core_peer,
            device_id_type=MESH,
        )

    for index in range(CHUNKS):
        proj_line(index).start()

    load_qn.wait()
    load_qr.wait()
    load_key.wait()

    def up(group, carry):
        for part in range(GROUP):
            columns = pl.ds(pl.multiple_of((group * GROUP + part) * NOPE, NOPE), NOPE)
            made = lax.dot_general(
                qn_ref[:, columns], key_up[:, columns], NT, preferred_element_type=jnp.float32
            ).astype(jnp.bfloat16)
            for half in range(SPLIT):
                query[half * groups + group, pl.ds(part * sub, sub), pl.ds(0, LATENT)] = made[
                    half * sub : (half + 1) * sub
                ]
        for pair in range(GROUP // 2):
            start = pl.multiple_of((group * (GROUP // 2) + pair) * 2 * ROPE, 2 * ROPE)
            both = rotated(qr_ref[:, pl.ds(start, 2 * ROPE)])
            for part, turned in ((0, both), (1, pltpu.roll(both, ROPE, 1))):
                rows = pl.ds((2 * pair + part) * sub, sub)
                turned = turned.astype(jnp.bfloat16)
                for half in range(SPLIT):
                    query[half * groups + group, rows, pl.ds(LATENT, KEYW - LATENT)] = turned[
                        half * sub : (half + 1) * sub
                    ]
        return carry

    lax.fori_loop(0, groups, up, 0)

    def kv_wait(origin):
        kv_copy(kv.at[origin], origin, kv_send_y.at[0], line_peer).wait_recv()

    def earlier(step):
        return lax.rem(z + n_z - step, n_z)

    for step in range(1, n_z):
        origin = ctx_of(earlier(step), line, core)
        allowed = z >= step
        pl.when(allowed)(functools.partial(kv_wait, origin))
        send_if(allowed, origin, kv_send_y.at[step], line_peer)
        send_if(allowed, origin, kv_send_c.at[0, step], core_peer)
    for step in range(n_z):
        origin = ctx_of(earlier(step), other_line, core)
        allowed = z >= step
        pl.when(allowed)(functools.partial(kv_wait, origin))
        send_if(allowed, origin, kv_send_c.at[1, step], core_peer)
    proj_core.start()
    for step in range(n_z):
        for line_at in (line, other_line):
            origin = ctx_of(earlier(step), line_at, 1 - core)
            pl.when(z >= step)(functools.partial(kv_wait, origin))
    load_value.wait()

    above = z + 1 < n_z
    below = z >= 1
    up_peer = (ctx_of(lax.rem(z + 1, n_z), line, core), head)
    down_peer = (ctx_of(lax.rem(z + n_z - 1, n_z), line, core), head)

    def ho_copy(way, time, z_at, there):
        return pltpu.make_async_remote_copy(
            src_ref=ho.at[time, z_at],
            dst_ref=ho.at[time, z_at],
            send_sem=ho_send_z.at[way, time, z_at],
            recv_sem=ho_recv.at[time, z_at],
            device_id=there,
            device_id_type=MESH,
        )

    def up_copy(time, z_at):
        return ho_copy(0, time, z_at, up_peer)

    def down_copy(time, z_at):
        return ho_copy(1, time, z_at, down_peer)

    scale = math.log2(math.e) / math.sqrt(NOPE + ROPE)
    n_rows = GROUP * sub

    def attend(time, blocks):
        half = time // groups
        group = lax.rem(time, groups)
        n_keys = blocks * tokens
        keys = kv[pl.ds(0, blocks)].reshape(n_keys, KEYW)
        scores = lax.dot_general(query[time], keys, NT, preferred_element_type=jnp.float32)
        row = lax.broadcasted_iota(jnp.int32, (n_rows, 1), 0)
        last = me * tokens + half * sub + lax.rem(row, sub)
        key_index = lax.broadcasted_iota(jnp.int32, (n_rows, n_keys), 1)
        scores = jnp.where(key_index <= last, scores, masked_value)
        peak = jnp.max(scores, axis=1, keepdims=True)
        weights = jnp.exp2((scores - peak) * scale)
        totals = jnp.sum(weights, axis=1, keepdims=True)
        summed = jnp.dot(
            weights.astype(jnp.bfloat16), keys[:, :LATENT], preferred_element_type=jnp.float32
        )
        latent_out = (summed * (1.0 / totals)).astype(jnp.bfloat16)
        for part in range(GROUP):
            columns = pl.ds(pl.multiple_of((group * GROUP + part) * VDIM, VDIM), VDIM)
            ho[time, z, :, pl.ds(part * VDIM, VDIM)] = jnp.dot(
                latent_out[part * sub : (part + 1) * sub],
                value_up[:, columns],
                preferred_element_type=jnp.float32,
            ).astype(jnp.bfloat16)

    def tick(time, carry):
        @pl.when(time < ticks)
        def _():
            pl.when(2 * z < n_z)(functools.partial(attend, time, n_ctx // 2))
            pl.when(2 * z >= n_z)(functools.partial(attend, time, n_ctx))
            pl.when(above)(lambda: up_copy(time, z).start())
            pl.when(below)(lambda: down_copy(time, z).start())

        for step in range(1, n_z - 1):
            past = time - step - LAG
            in_time = jnp.logical_and(past >= 0, past < ticks)

            @pl.when(jnp.logical_and(in_time, jnp.logical_and(z >= step, above)))
            def _():
                up_copy(past, z - step).wait_recv()
                up_copy(past, z - step).start()

            @pl.when(jnp.logical_and(in_time, jnp.logical_and(z + step < n_z, below)))
            def _():
                down_copy(past, z + step).wait_recv()
                down_copy(past, z + step).start()

        return carry

    lax.fori_loop(0, ticks + n_z - 2 + LAG, tick, 0)

    for index in range(CHUNKS):
        proj_line(index).wait_recv()
        proj_across(index).start()
    load_proj.wait()
    proj_core.wait_recv()
    for index in range(CHUNKS):
        proj_across(index).wait_recv()

    def back(half, z_at):
        return pltpu.make_async_remote_copy(
            src_ref=out_send.at[half, z_at],
            dst_ref=land.at[head, slot, half],
            send_sem=back_send.at[half, z_at],
            recv_sem=land_recv.at[head, slot, half],
            device_id=(ctx_of(z_at, line, core), owner_head),
            device_id_type=MESH,
        )

    stays = owner_head == head

    for half in range(SPLIT):
        acc[...] = jnp.zeros_like(acc)

        def add(group, carry):
            time = half * groups + group
            for step in range(1, n_z):

                @pl.when(jnp.logical_and(z >= step, jnp.logical_or(z == n_z - 1, step == n_z - 1)))
                def _():
                    up_copy(time, z - step).wait_recv()

                @pl.when(jnp.logical_and(z + step < n_z, jnp.logical_or(z == 0, step == n_z - 1)))
                def _():
                    down_copy(time, z + step).wait_recv()

            block = ho[time].reshape(n_z * sub, GROUP * VDIM)
            span = pl.ds(pl.multiple_of(group * (GROUP * VDIM), GROUP * VDIM), GROUP * VDIM)
            for line_at in range(LINES):
                for core_at in range(CORES):
                    acc[line_at, core_at] += lax.dot_general(
                        block,
                        proj[line_at, core_at, :, span],
                        NT,
                        preferred_element_type=jnp.float32,
                    )
            return carry

        lax.fori_loop(0, groups, add, 0)
        for z_at in range(n_z):
            out_send[half, z_at] = acc[:, :, pl.ds(z_at * sub, sub), :].astype(jnp.bfloat16)
        for step in range(1, n_z):
            back(half, z_peer(step)).start()

        @pl.when(stays)
        def _():
            pltpu.make_async_copy(
                out_send.at[half, z], land.at[head, slot, half], land_recv.at[head, slot, half]
            ).start()

        @pl.when(jnp.logical_not(stays))
        def _():
            back(half, z).start()

    for half in range(SPLIT):
        for part in range(n_head):
            for spot in range(spots):
                pltpu.make_async_copy(
                    out_send.at[0, 0], land.at[part, spot, half], land_recv.at[part, spot, half]
                ).wait()
        columns = []
        for spot in range(spots):
            for line_at in range(LINES):
                for core_at in range(CORES):
                    total = land[0, spot, half, line_at, core_at].astype(jnp.float32)
                    for part in range(1, n_head):
                        total += land[part, spot, half, line_at, core_at].astype(jnp.float32)
                    columns.append(total)
        out_ref[pl.ds(half * sub, sub), :] = jnp.concatenate(columns, axis=1).astype(out_ref.dtype)

    for allowed, copy in sends:
        if allowed is None:
            copy.wait_send()
        else:
            pl.when(allowed)(copy.wait_send)
    proj_core.wait_send()
    for index in range(CHUNKS):
        proj_line(index).wait_send()
        proj_across(index).wait_send()

    def drain(time, carry):
        for z_at in range(n_z):
            pl.when(jnp.logical_and(above, z >= z_at))(up_copy(time, z_at).wait_send)
            pl.when(jnp.logical_and(below, z <= z_at))(down_copy(time, z_at).wait_send)
        return carry

    lax.fori_loop(0, ticks, drain, 0)
    for half in range(SPLIT):
        for step in range(1, n_z):
            back(half, z_peer(step)).wait_send()
        pl.when(jnp.logical_not(stays))(back(half, z).wait_send)


def body(
    n_ctx,
    n_head,
    queries_nope,
    queries_rope,
    latents,
    rope_keys,
    positions,
    key_up,
    value_up,
    out_proj,
):
    tokens = latents.shape[0]
    heads = key_up.shape[1] // NOPE
    groups = heads // GROUP
    n_z = n_ctx // (CORES * LINES)
    spots = n_z // n_head
    sub = tokens // SPLIT
    width = out_proj.shape[1]
    bf16 = jnp.bfloat16
    cosine, sine = rope_tables(positions, ROPE)
    cosine = jnp.concatenate([cosine] * 4, axis=1)
    sine = jnp.concatenate([-sine, sine] * 2, axis=1)
    out_proj = out_proj.T
    vmem = pl.BlockSpec(memory_space=pltpu.VMEM)
    hbm = pl.BlockSpec(memory_space=pltpu.HBM)
    dma = pltpu.SemaphoreType.DMA
    rows = n_ctx * tokens * heads * tokens
    return pl.pallas_call(
        functools.partial(kernel, n_ctx, n_head),
        out_shape=jax.ShapeDtypeStruct((tokens, spots * LINES * CORES * width), bf16),
        in_specs=[hbm] * 2 + [vmem] * 2 + [hbm] * 5,
        out_specs=vmem,
        scratch_shapes=[
            pltpu.VMEM(latents.shape, bf16),
            pltpu.VMEM(rope_keys.shape, bf16),
            pltpu.VMEM((tokens, KEYW - LATENT), jnp.float32),
            pltpu.VMEM(queries_nope.shape, bf16),
            pltpu.VMEM(queries_rope.shape, bf16),
            pltpu.VMEM(key_up.shape, bf16),
            pltpu.VMEM(value_up.shape, bf16),
            pltpu.VMEM((LINES, CORES) + out_proj.shape, bf16),
            pltpu.VMEM((n_ctx, tokens, KEYW), bf16),
            pltpu.VMEM((SPLIT * groups, GROUP * sub, KEYW), bf16),
            pltpu.VMEM((SPLIT * groups, n_z, sub, GROUP * VDIM), bf16),
            pltpu.VMEM((LINES, CORES, n_z * sub, width), jnp.float32),
            pltpu.VMEM((SPLIT, n_z, LINES, CORES, sub, width), bf16),
            pltpu.VMEM((n_head, spots, SPLIT, LINES, CORES, sub, width), bf16),
            dma((7,)),
            dma,
            dma((CHUNKS,)),
            dma((CHUNKS,)),
            dma,
            dma((CHUNKS,)),
            dma((CHUNKS,)),
            dma((n_z,)),
            dma((n_z,)),
            dma((LINES, n_z)),
            dma((n_ctx,)),
            dma((2, SPLIT * groups, n_z)),
            dma((SPLIT * groups, n_z)),
            dma((SPLIT, n_z)),
            dma((n_head, spots, SPLIT)),
        ],
        compiler_params=pltpu.CompilerParams(
            collective_id=0, has_side_effects=True, vmem_limit_bytes=52 * 1024 * 1024
        ),
        cost_estimate=pl.CostEstimate(
            flops=2 * rows * (KEYW + LATENT), bytes_accessed=1 << 24, transcendentals=rows
        ),
    )(latents, rope_keys, cosine, sine, queries_nope, queries_rope, key_up, value_up, out_proj)


def solution(mesh):
    in_specs = (
        P("ctx", "head"),
        P("ctx", "head"),
        P("ctx", None),
        P("ctx", None),
        P("ctx"),
        P(None, "head"),
        P(None, "head"),
        P("head", "ctx"),
    )
    out_specs = P("ctx", "head")
    run = functools.partial(body, mesh.shape["ctx"], mesh.shape["head"])
    return jax.shard_map(run, mesh=mesh, in_specs=in_specs, out_specs=out_specs, check_vma=False)
```

profile of v0, /device:TPU:3, one launch (start us, length us, event | category | flops | bytes accessed | tf_op | source)
XLA Modules:
  0.0 104.4 jit_solution(12010593072319898745)
XLA Ops:
  0.0 0.7 convert_element_type.3
  0.7 0.2 fusion
  0.9 0.1 pad_maximum_fusion
  1.0 0.0 copy-start
  1.0 1.0 copy-done
  2.0 0.0 copy-start.1
  2.0 0.9 copy-done.1
  3.0 0.0 copy-start.2
  3.0 0.8 copy-done.2
  3.8 0.0 copy-start.3
  3.8 0.7 copy-done.3
  4.6 99.1 %shard_map.82 = bf16[64,1792]{1,0:T(8,128)(2,1)S(1)} custom-call(bf16[64,512]{1,0:T(8,128)(2,1)S(1)} %copy-done.2, bf16[64,64]{1,0:T(8,128)(2,1)S(1)} %copy-done.3, f32[64,128]{1,0:T(8,128)S(1)} %get-tuple-element.8.cos_ref, f32[64,128]{1,0:T(8,128)S(1)} %get-tuple-element.9.sin_ref, bf16[64,4096]{1,0:T(8,128)(2,1)S(1)} %copy-done, ...), custom_call_target="tpu_custom_call" | custom-call | flops 4831838208 | bytes 16777216 | tf_op jit(solution)/shard_map/pallas_call | solution.py:473
  103.7 0.7 copy.10
  (1 shorter events, 0.0 us)
Async XLA Ops:
  1.0 1.0 %copy-start = (bf16[64,4096]{1,0:T(8,128)(2,1)S(1)}, bf16[64,4096]{1,0:T(8,128)(2,1)}, u32[]{:S(2)}) copy-start(bf16[64,4096]{1,0:T(8,128)(2,1)} %qn_hbm.1) | copy-start | bytes 1572868
  2.0 0.9 copy-start.1
  3.0 0.8 copy-start.2
  3.8 0.7 copy-start.3
where the time goes:
time: 106 us; the launch traced here: 104 us
  Pallas kernels  99.1 us (93%)
  local copies, waits for them, and re-layouts  4.23 us (4%)
    pallas_call x1, Pallas kernels, body(): pl.pallas_call(functools.partial(kernel, n_ctx, n_head), out_shape=jax.Sh...  99.1 us
    unnamed x9, local copies, waits for them, and re-layouts  4.23 us

commit v1 on v0

--- a/solution.py
+++ b/solution.py
@@ -210,9 +210,6 @@
             device_id_type=MESH,
         )
 
-    for index in range(CHUNKS):
-        proj_line(index).start()
-
     load_qn.wait()
     load_qr.wait()
     load_key.wait()
@@ -253,6 +250,8 @@
         pl.when(allowed)(functools.partial(kv_wait, origin))
         send_if(allowed, origin, kv_send_y.at[step], line_peer)
         send_if(allowed, origin, kv_send_c.at[0, step], core_peer)
+    for index in range(CHUNKS):
+        proj_line(index).start()
     for step in range(n_z):
         origin = ctx_of(earlier(step), other_line, core)
         allowed = z >= step
@@ -467,7 +466,7 @@
     sine = jnp.concatenate([-sine, sine] * 2, axis=1)
     out_proj = out_proj.T
     vmem = pl.BlockSpec(memory_space=pltpu.VMEM)
-    hbm = pl.BlockSpec(memory_space=pltpu.HBM)
+    hbm = pl.BlockSpec(memory_space=pl.ANY)
     dma = pltpu.SemaphoreType.DMA
     rows = n_ctx * tokens * heads * tokens
     return pl.pallas_call(

time: 106 us -> 76.9 us (0.73)
  Pallas kernels: 99.1 us -> 70.3 us
    pallas_call x1, Pallas kernels: 99.1 us -> 70.3 us  [body(): pl.pallas_call(functools.partial(kernel, n_ctx, n_head), out_shape=jax.Sh...]
where the time goes in v1:
time: 76.9 us; the launch traced here: 75.5 us
  Pallas kernels  70.3 us (91%)
  local copies, waits for them, and re-layouts  4.23 us (6%)
  other arithmetic  0.98 us (1%)
    pallas_call x1, Pallas kernels, body(): pl.pallas_call(functools.partial(kernel, n_ctx, n_head), out_shape=jax.Sh...  70.3 us
    unnamed x9, local copies, waits for them, and re-layouts  4.23 us

profile of v1, /device:TPU:3, one launch (start us, length us, event | category | flops | bytes accessed | tf_op | source)
XLA Modules:
  0.0 75.5 jit_solution(9226004699926842594)
XLA Ops:
  0.0 0.7 convert_element_type.3
  0.7 0.2 fusion
  0.9 0.1 pad_maximum_fusion
  1.0 0.0 copy-start
  1.0 1.0 %copy-done = bf16[64,4096]{1,0:T(8,128)(2,1)S(1)} copy-done((bf16[64,4096]{1,0:T(8,128)(2,1)S(1)}, bf16[64,4096]{1,0:T(8,128)(2,1)}, u32[]{:S(2)}) %copy-start) | copy-done | bytes 524312
  2.0 0.0 copy-start.1
  2.0 0.9 %copy-done.1 = bf16[64,2048]{1,0:T(8,128)(2,1)S(1)} copy-done((bf16[64,2048]{1,0:T(8,128)(2,1)S(1)}, bf16[64,2048]{1,0:T(8,128)(2,1)}, u32[]{:S(2)}) %copy-start.1) | copy-done | bytes 262168
  3.0 0.0 copy-start.2
  3.0 0.8 %copy-done.2 = bf16[64,512]{1,0:T(8,128)(2,1)S(1)} copy-done((bf16[64,512]{1,0:T(8,128)(2,1)S(1)}, bf16[64,512]{1,0:T(8,128)(2,1)}, u32[]{:S(2)}) %copy-start.2) | copy-done | bytes 65560
  3.8 0.0 copy-start.3
  3.8 0.7 copy-done.3
  4.6 70.3 %shard_map.82 = bf16[64,1792]{1,0:T(8,128)(2,1)S(1)} custom-call(bf16[64,512]{1,0:T(8,128)(2,1)S(1)} %copy-done.2, bf16[64,64]{1,0:T(8,128)(2,1)S(1)} %copy-done.3, f32[64,128]{1,0:T(8,128)S(1)} %get-tuple-element.8.cos_ref, f32[64,128]{1,0:T(8,128)S(1)} %get-tuple-element.9.sin_ref, bf16[64,4096]{1,0:T(8,128)(2,1)S(1)} %copy-done, ...), custom_call_target="tpu_custom_call" | custom-call | flops 4831838208 | bytes 16777216 | tf_op jit(solution)/shard_map/pallas_call | solution.py:472
  74.8 0.7 copy.10
  (1 shorter events, 0.0 us)
Async XLA Ops:
  1.0 1.0 %copy-start = (bf16[64,4096]{1,0:T(8,128)(2,1)S(1)}, bf16[64,4096]{1,0:T(8,128)(2,1)}, u32[]{:S(2)}) copy-start(bf16[64,4096]{1,0:T(8,128)(2,1)} %qn_hbm.1) | copy-start | bytes 1572868
  2.0 0.9 %copy-start.1 = (bf16[64,2048]{1,0:T(8,128)(2,1)S(1)}, bf16[64,2048]{1,0:T(8,128)(2,1)}, u32[]{:S(2)}) copy-start(bf16[64,2048]{1,0:T(8,128)(2,1)} %qr_hbm.1) | copy-start | bytes 786436
  3.0 0.8 %copy-start.2 = (bf16[64,512]{1,0:T(8,128)(2,1)S(1)}, bf16[64,512]{1,0:T(8,128)(2,1)}, u32[]{:S(2)}) copy-start(bf16[64,512]{1,0:T(8,128)(2,1)} %lat_hbm.1) | copy-start | bytes 196612
  3.8 0.7 copy-start.3
